TPU v7x, 32 devices: a whole 2x2x4 slice. The times are simulated.
32 devices in a mesh: groups: 1, ep: 16 (over z, y, x), side: 2 (over core).
Axes of the slice: x: 2, y: 2, z: 4, core: 2. Of those that a mesh axis runs over, the one named last changes fastest.
Arguments:
- queries: bfloat16 [64, 36864], P(('groups', 'ep', 'side')), may hold values from -60 to 60
- latents: bfloat16 [64, 576, 512], P(('groups', 'ep', 'side')), may hold values from -4.5 to 4.5
- lengths: int32 [64], P(('groups', 'ep', 'side')), may hold values from 64 to 512, as said below
- tokens: bfloat16 [1024, 3584], P(('groups', 'ep', 'side')), may hold values from -30 to 30
- routes: int32 [1024, 8], P(('groups', 'ep', 'side')), may hold values from 0 to 15, all different within a row; in each aligned block of 32 rows (0 to 31, 32 to 63, ...) at most 32 rows name the same one
- router: bfloat16 [3584, 16], replicated, may hold values from -0.09375 to 0.09375
- gate_weight: bfloat16 [16, 3584, 1024], P('ep', None, 'side'), may hold values from -0.09375 to 0.09375
- up_weight: bfloat16 [16, 3584, 1024], P('ep', None, 'side'), may hold values from -0.09375 to 0.09375
- down_weight: bfloat16 [16, 1024, 3584], P('ep', 'side'), may hold values from -0.1875 to 0.1875
Outputs:
- attended: bfloat16 [64, 32768], P(('groups', 'ep', 'side'))
- moe: bfloat16 [1024, 3584], P(('groups', 'ep', 'side'))
Inputs may be any that keep to these rules, and one draw needn't show every extreme that they name: `lengths`: some request of every draw has all 512 positions live. `routes`: among the rows of one device, no expert is named by more than 32 rows, a bound that some block reaches.
All inputs are finite; a program needn't handle non-finite values.
Results may differ from a plain program's by a relative error of at most 0.0072.
Values may be sent and summed in bfloat16 or wider, within the bound.
A program may use at most 128 MiB of HBM per device.

v0:
```python
import jax
import jax.numpy as jnp
from jax import lax
from jax.sharding import PartitionSpec as P

LATENT = 512


SOFT_SCALE = 192.0 ** (-0.5)
ROUTE_SCALE = 2.5
NORM_EPS = 1e-06


def attend_request(query_row, cache_block, length):
    positions = cache_block.shape[1]
    head_queries = query_row.reshape(-1, cache_block.shape[0])
    scores = jnp.dot(head_queries, cache_block, preferred_element_type=jnp.float32) * SOFT_SCALE
    live = lax.broadcasted_iota(jnp.int32, (1, positions), 1) < length
    scores = jnp.where(live, scores, -1e30)
    highest = jnp.max(scores, axis=1, keepdims=True)
    powers = jnp.where(live, jnp.exp(scores - highest), 0.0)
    probs = (powers / jnp.sum(powers, axis=1, keepdims=True)).astype(jnp.bfloat16)
    mixed = lax.dot_general(
        probs, cache_block[:LATENT], (((1,), (1,)), ((), ())), preferred_element_type=jnp.float32
    )
    return mixed.astype(jnp.bfloat16).reshape(-1)


def expert_block(rows, gate_matrix, up_matrix, down_matrix):
    gate = jnp.dot(rows, gate_matrix, preferred_element_type=jnp.float32)
    up = jnp.dot(rows, up_matrix, preferred_element_type=jnp.float32)
    hidden = (jax.nn.silu(gate) * up).astype(jnp.bfloat16)
    return jnp.dot(hidden, down_matrix, preferred_element_type=jnp.float32)


def expert_rows(rows, valid, gate_matrix, up_matrix, down_matrix):
    return jnp.where(valid[:, None], expert_block(rows, gate_matrix, up_matrix, down_matrix), 0.0)


def slot_mask(counts, capacity):
    return (
        lax.broadcasted_iota(jnp.int32, (counts.shape[0], capacity), 1) < counts[:, None]
    ).reshape(-1)


def body(queries, latents, lengths, tokens, routes, router, gate_weight, up_weight, down_weight):
    attended = jax.vmap(attend_request)(queries, latents, lengths)
    experts = lax.axis_size("ep")
    token_count, top_count = routes.shape
    width = tokens.shape[1]
    capacity = min(token_count, 2 * token_count * top_count // experts)
    values = tokens.astype(jnp.float32)
    mean_square = jnp.mean(values * values, axis=1, keepdims=True)
    normed = (values * lax.rsqrt(mean_square + NORM_EPS)).astype(jnp.bfloat16)
    affinity = jax.nn.sigmoid(jnp.dot(normed, router, preferred_element_type=jnp.float32))
    one_hot = routes[:, :, None] == lax.broadcasted_iota(jnp.int32, (1, 1, experts), 2)
    chosen = jnp.sum(jnp.where(one_hot, affinity[:, None, :], 0.0), axis=2)
    gates = chosen / jnp.sum(chosen, axis=1, keepdims=True) * ROUTE_SCALE
    flat_hot = one_hot.reshape(-1, experts).astype(jnp.int32)
    slot = jnp.sum((jnp.cumsum(flat_hot, axis=0) - flat_hot) * flat_hot, axis=1)
    counts = jnp.sum(flat_hot, axis=0)
    target = routes.reshape(-1) * capacity + slot
    outgoing = (
        jnp.zeros((experts * capacity, width), jnp.bfloat16)
        .at[target]
        .set(jnp.repeat(normed, top_count, axis=0))
    )
    outgoing = outgoing.reshape(experts, capacity, width)
    gate_matrix = gate_weight[0]
    up_matrix = up_weight[0]
    down_matrix = down_weight[0]
    arrived, arrived_counts = (
        lax.all_to_all(outgoing, "ep", split_axis=0, concat_axis=0, tiled=True),
        lax.all_to_all(counts, "ep", split_axis=0, concat_axis=0, tiled=True),
    )
    paired, paired_counts = (
        lax.all_gather(arrived, "side", axis=0, tiled=True),
        lax.all_gather(arrived_counts, "side", axis=0, tiled=True),
    )
    paired_rows = paired.reshape(-1, width)
    valid = slot_mask(paired_counts, capacity)
    summed = lax.psum_scatter(
        expert_rows(paired_rows, valid, gate_matrix, up_matrix, down_matrix),
        "side",
        scatter_dimension=0,
        tiled=True,
    )
    returned = lax.all_to_all(
        summed.astype(jnp.bfloat16).reshape(experts, capacity, width),
        "ep",
        split_axis=0,
        concat_axis=0,
        tiled=True,
    )
    picked = returned.reshape(experts * capacity, width)[target]
    weighted = picked.reshape(token_count, top_count, width).astype(jnp.float32) * gates[:, :, None]
    moe = jnp.sum(weighted, axis=1)
    return (attended, moe.astype(jnp.bfloat16))


def solution(mesh):
    return jax.shard_map(
        body,
        mesh=mesh,
        in_specs=(
            P(("groups", "ep", "side"), None),
            P(("groups", "ep", "side"), None, None),
            P(("groups", "ep", "side")),
            P(("groups", "ep", "side"), None),
            P(("groups", "ep", "side"), None),
            P(),
            P("ep", None, "side"),
            P("ep", None, "side"),
            P("ep", "side", None),
        ),
        out_specs=(P(("groups", "ep", "side"), None), P(("groups", "ep", "side"), None)),
        check_vma=False,
    )
```

profile of v0, /device:TPU:14, one launch (start us, length us, event | category | flops | bytes accessed | tf_op | source)
XLA Modules:
  0.0 283.5 jit_solution(11965931386023255613)
XLA Ops:
  7.2 0.7 broadcast_multiply_fusion
  7.9 0.8 copy.33
  8.9 1.1 fusion.25
  10.0 0.1 mul.65
  10.1 0.6 reduce-window.6
  10.7 0.2 slice_reduce_fusion
  11.0 1.1 fusion.26
  12.0 0.1 fusion.29
  12.2 5.5 %scatter_custom_fusion = bf16[512,3584]{1,0:T(8,128)(2,1)} fusion(s32[256]{0:T(256)S(1)} %bitcast.51, bf16[]{:T(256)} %constant.7.clone.1, bf16[32,3584]{1,0:T(8,128)(2,1)S(1)} %fusion.26), kind=kCustom, calls=%fused_computation.12 | custom fusion | bytes 3899394 | tf_op jit(solution)/shard_map/scatter | solution.py:66
  17.7 87.7 %all_to_all.22 = bf16[16,32,3584]{2,1,0:T(8,128)(2,1)} all-to-all(bf16[16,32,3584]{2,1,0:T(8,128)(2,1)} %bitcast.48), channel_id=1, replica_groups=mesh['groups'=1,'ep'=16,'side'=2] {'ep'}, dimensions={0} | all-to-all | bytes 7340032 | tf_op jit(solution)/shard_map/all_to_all | solution.py:73
  105.4 0.7 copy.34
  106.0 6.0 %all-to-all-start = ((s32[16,1,1]{2,1,0:T(1,128)}), s32[16,1,1]{2,1,0:T(1,128)S(1)}, u32[]{:S(2)}, u32[]{:S(2)}) async-start(s32[16,1,1]{2,1,0:T(1,128)} %copy.34), calls=%async_computation | async-start | bytes 16384 | tf_op jit(solution)/shard_map/all_to_all | solution.py:74
  112.1 0.6 dynamic-slice
  113.4 2.7 all-to-all-done
  116.1 0.4 reduce.1
  116.5 0.2 dynamic-update-slice
  116.7 1.8 all-reduce
  118.6 0.1 lt.49
  118.7 5.3 %all-gather.3.cloned.1.call-done = bf16[32,32,3584]{2,1,0:T(8,128)(2,1)} async-done(((bf16[16,32,3584]{2,1,0:T(8,128)(2,1)}), bf16[32,32,3584]{2,1,0:T(8,128)(2,1)}) %all-gather.3.cloned.1.call-update) | async-done | bytes 7340048 | tf_op jit(solution)/shard_map/all_gather | solution.py:77
  124.0 7.3 %fusion.3 = f32[1024,512]{1,0:T(8,128)S(1)} fusion(bf16[1024,3584]{1,0:T(8,128)(2,1)} %bitcast.55, bf16[1,3584,512]{2,1,0:T(8,128)(2,1)} %param.16), kind=kOutput, calls=%fused_computation.7 | convolution fusion | flops 3758096384 | bytes 13107200 | tf_op jit(solution)/shard_map/dot_general | solution.py:31
  131.3 15.5 %convolution_select_fusion = f32[1024,3584]{1,0:T(8,128)} fusion(pred[1024]{0:T(1024)(128)(4,1)S(1)} %lt.49, bf16[1,512,3584]{2,1,0:T(8,128)(2,1)} %param.17, f32[1024,512]{1,0:T(8,128)S(1)} %fusion.3, bf16[1024,3584]{1,0:T(8,128)(2,1)} %bitcast.56, bf16[1,3584,512]{2,1,0:T(8,128)(2,1)} %param.15), kind=kOutput, calls=%fused_computation.3 | convolution fusion | flops 7523008512 | bytes 31458304 | tf_op jit(solution)/shard_map/dot_general | solution.py:33
  146.9 25.3 %reduce-scatter.2.cloned.1.call-done = f32[512,3584]{1,0:T(8,128)} async-done(((f32[1024,3584]{1,0:T(8,128)}), f32[512,3584]{1,0:T(8,128)}) %reduce-scatter.2.cloned.1.call-update) | async-done | bytes 7340048 | tf_op jit(solution)/shard_map/reduce_scatter | solution.py:82
  172.2 5.3 %convert_element_type.41 = bf16[512,3584]{1,0:T(8,128)(2,1)} convert(f32[512,3584]{1,0:T(8,128)} %reduce-scatter.2.cloned.1.call-done) | non-fusion elementwise | flops 1835008 | bytes 11010048 | tf_op jit(solution)/shard_map/convert_element_type | solution.py:89
  177.5 7.1 %all-to-all-start.2 = ((bf16[16,32,3584]{2,1,0:T(8,128)(2,1)}), bf16[16,32,3584]{2,1,0:T(8,128)(2,1)}, u32[]{:S(2)}, u32[]{:S(2)}) async-start(bf16[16,32,3584]{2,1,0:T(8,128)(2,1)} %bitcast.49), calls=%async_computation.3 | async-start | bytes 7340032 | tf_op jit(solution)/shard_map/all_to_all | solution.py:88
  184.6 0.2 reshape.143
  184.9 0.5 fusion.32
  185.4 0.5 fusion.18
  185.9 0.8 copy.40
  186.7 0.2 fusion.21
  187.0 81.5 %all-to-all-done.2 = bf16[16,32,3584]{2,1,0:T(8,128)(2,1)} async-done(((bf16[16,32,3584]{2,1,0:T(8,128)(2,1)}), bf16[16,32,3584]{2,1,0:T(8,128)(2,1)}, u32[]{:S(2)}, u32[]{:S(2)}) %all-to-all-start.2) | async-done | bytes 3670048 | tf_op jit(solution)/shard_map/all_to_all | solution.py:88
  268.5 6.0 %gather_fusion = bf16[256,3584]{1,0:T(8,128)(2,1)S(1)} fusion(bf16[512,3584]{1,0:T(8,128)(2,1)} %bitcast.12, s32[1024]{0:T(1024)S(1)} %pad_clamp_fusion), kind=kCustom, calls=%fused_computation | custom fusion | bytes 3671040 | tf_op jit(solution)/shard_map/gather | solution.py:95
  274.5 2.1 fusion.1
  (31 shorter events, 0.7 us)
Async XLA Ops:
  7.2 179.5 %copy-start = (bf16[3584,16]{0,1:T(8,128)(2,1)S(1)}, bf16[3584,16]{0,1:T(8,128)(2,1)}, u32[]{:S(2)}) copy-start(bf16[3584,16]{0,1:T(8,128)(2,1)} %param.14) | copy-start | bytes 344068
  7.2 116.9 %all-gather.3.cloned.1.call-start = ((), (), s32[]{:S(2)}) async-start(), calls=%async_computation.4 | async-start | bytes 11010048 | tf_op jit(solution)/shard_map/all_gather | solution.py:77
  105.3 6.8 %copy-start.5 = (u32[32]{0:T(128)S(1)}, u32[32]{0:T(128)}, u32[]{:S(2)}) copy-start(u32[32]{0:T(128)} %constant.40) | copy-start | bytes 388
  106.0 10.1 %all-to-all-start = ((s32[16,1,1]{2,1,0:T(1,128)}), s32[16,1,1]{2,1,0:T(1,128)S(1)}, u32[]{:S(2)}, u32[]{:S(2)}) async-start(s32[16,1,1]{2,1,0:T(1,128)} %copy.34), calls=%async_computation | async-start | bytes 16384 | tf_op jit(solution)/shard_map/all_to_all | solution.py:74
  112.0 60.2 %reduce-scatter.2.cloned.1.call-start = ((), (), s32[]{:S(2)}) async-start(), calls=%async_computation.5 | async-start | bytes 22020096 | tf_op jit(solution)/shard_map/reduce_scatter | solution.py:82
  177.5 7.1 %copy-start.2 = (bf16[2,36864]{1,0:T(2,128)(2,1)S(1)}, bf16[2,36864]{1,0:T(2,128)(2,1)}, u32[]{:S(2)}) copy-start(bf16[2,36864]{1,0:T(2,128)(2,1)} %param.9) | copy-start | bytes 442372
  177.5 7.3 %copy-start.4 = (s32[2]{0:T(128)S(1)}, s32[2]{0:T(128)}, u32[]{:S(2)}) copy-start(s32[2]{0:T(128)} %param.11) | copy-start | bytes 28
  177.5 7.4 %copy-start.1 = (bf16[2,576,512]{2,1,0:T(8,128)(2,1)S(1)}, bf16[2,576,512]{2,1,0:T(8,128)(2,1)}, u32[]{:S(2)}) copy-start(bf16[2,576,512]{2,1,0:T(8,128)(2,1)} %param.10) | copy-start | bytes 3538948
  177.5 91.0 %all-to-all-start.2 = ((bf16[16,32,3584]{2,1,0:T(8,128)(2,1)}), bf16[16,32,3584]{2,1,0:T(8,128)(2,1)}, u32[]{:S(2)}, u32[]{:S(2)}) async-start(bf16[16,32,3584]{2,1,0:T(8,128)(2,1)} %bitcast.49), calls=%async_computation.3 | async-start | bytes 7340032 | tf_op jit(solution)/shard_map/all_to_all | solution.py:88
  184.6 2.3 copy-start.3
Sparse Core Ops, SparseCore 0:
  105.5 18.5 all-gather.2
  147.0 25.1 reduce-scatter.1
where the time goes:
time: 284 us
  waiting for transfers between devices  115 us (40%)
  blocking collectives  89.5 us (32%)
  matrix products  24 us (8%)
  local copies, waits for them, and re-layouts  15.5 us (5%)
  between operations  14.8 us (5%)
  starting transfers between devices  13.2 us (5%)
  other arithmetic  11.6 us (4%)
    all_to_all x1, blocking collectives, body(): lax.all_to_all(outgoing, 'ep', split_axis=0, concat_axis=0, tiled=True)  87.7 us
    all_to_all x1, waiting for transfers between devices, body(): lax.all_to_all(summed.astype(jnp.bfloat16).reshape(experts, capacity, wid...  81.5 us
    reduce_scatter x1, waiting for transfers between devices, body(): lax.psum_scatter(expert_rows(paired_rows, valid, gate_matrix, up_matrix,...  25.3 us
    dot_general x1, matrix products, expert_block(): return jnp.dot(hidden, down_matrix, preferred_element_type=jnp.float32)  15.5 us
    dot_general x1, matrix products, expert_block(): up = jnp.dot(rows, up_matrix, preferred_element_type=jnp.float32)  7.29 us
    all_to_all x1, starting transfers between devices, body(): lax.all_to_all(summed.astype(jnp.bfloat16).reshape(experts, capacity, wid...  7.09 us
    gather x1, local copies, waits for them, and re-layouts, body(): picked = returned.reshape(experts * capacity, width)[target]  6.04 us
    all_to_all x1, starting transfers between devices, body(): lax.all_to_all(counts, 'ep', split_axis=0, concat_axis=0, tiled=True)  6.01 us
  transfers between devices with their start and end apart: 4, of which 4 were waited for; matrix products, arithmetic and copies ran while one was open for 2% of the time, Pallas kernels for 0%

commit v1 on v0

--- a/solution.py
+++ b/solution.py
@@ -56,6 +56,20 @@
     one_hot = routes[:, :, None] == lax.broadcasted_iota(jnp.int32, (1, 1, experts), 2)
     chosen = jnp.sum(jnp.where(one_hot, affinity[:, None, :], 0.0), axis=2)
     gates = chosen / jnp.sum(chosen, axis=1, keepdims=True) * ROUTE_SCALE
+    if capacity == token_count:
+        both = ("ep", "side")
+        dense = jnp.sum(jnp.where(one_hot, gates[:, :, None], 0.0), axis=1)
+        rows = lax.all_gather(normed, both, axis=0, tiled=True)
+        shares = lax.all_gather(dense, both, axis=0, tiled=True)
+        share = lax.dynamic_slice_in_dim(shares, lax.axis_index("ep"), 1, 1)
+        gate = jnp.dot(rows, gate_weight[0], preferred_element_type=jnp.float32)
+        up = jnp.dot(rows, up_weight[0], preferred_element_type=jnp.float32)
+        hidden = (jax.nn.silu(gate) * up * share).astype(jnp.bfloat16)
+        partial = jnp.dot(hidden, down_weight[0], preferred_element_type=jnp.float32)
+        moe = lax.psum_scatter(
+            partial.astype(jnp.bfloat16), both, scatter_dimension=0, tiled=True
+        )
+        return (attended, moe)
     flat_hot = one_hot.reshape(-1, experts).astype(jnp.int32)
     slot = jnp.sum((jnp.cumsum(flat_hot, axis=0) - flat_hot) * flat_hot, axis=1)
     counts = jnp.sum(flat_hot, axis=0)

time: 284 us -> 263 us (0.926)
  the two profiles are of different devices: /device:TPU:14 before, /device:TPU:0 now
where the time goes in v1:
time: 263 us; the launch traced here: 262 us
  waiting for transfers between devices  173 us (66%)
  blocking collectives  44.3 us (17%)
  matrix products  23.8 us (9%)
  between operations  14.1 us (5%)
  other arithmetic  4.38 us (2%)
    reduce_scatter x1, waiting for transfers between devices, body(): lax.psum_scatter(partial.astype(jnp.bfloat16), both, scatter_dimension=0,...  142 us
    all_gather x1, blocking collectives, body(): shares = lax.all_gather(dense, both, axis=0, tiled=True)  44.3 us
    all_gather x1, waiting for transfers between devices, body(): rows = lax.all_gather(normed, both, axis=0, tiled=True)  30.8 us
    dot_general x1, matrix products, body(): jnp.dot(hidden, down_weight[0], preferred_element_type=jnp.float32)  14.4 us
    dot_general x1, matrix products, body(): up = jnp.dot(rows, up_weight[0], preferred_element_type=jnp.float32)  7.29 us
  transfers between devices with their start and end apart: 2, of which 2 were waited for; matrix products, arithmetic and copies ran while one was open for 2% of the time, Pallas kernels for 0%

profile of v1, /device:TPU:0, one launch (start us, length us, event | category | flops | bytes accessed | tf_op | source)
XLA Modules:
  0.0 262.3 jit_solution(2065265867801899084)
XLA Ops:
  7.2 0.0 copy-start
  7.2 0.0 all-gather.3.cloned.1.call-start
  7.2 1.1 fusion.21
  8.3 1.7 fusion.22
  10.1 0.0 all-gather.3.cloned.1.call-update
  10.1 0.0 reduce-scatter.2.cloned.1.call-start
  10.1 0.0 copy-done
  10.2 1.1 fusion.17
  11.3 0.8 select_reduce_fusion
  12.0 0.7 select_reduce_fusion.2
  12.7 44.3 %all-gather = f32[32,32,16]{1,2,0:T(8,128)S(1)} all-gather(f32[1,32,16]{1,2,0:T(8,128)S(1)} %bitcast.27), channel_id=1, replica_groups=mesh['groups'=1,'ep'=16,'side'=2] {'ep','side'}, dimensions={0}, use_global_device_ids=true | all-gather | bytes 67584 | tf_op jit(solution)/shard_map/all_gather | solution.py:63
  57.0 0.1 copy.20
  57.1 0.1 reshape.65
  57.2 30.8 %all-gather.3.cloned.1.call-done = bf16[1024,3584]{1,0:T(8,128)(2,1)} async-done(((bf16[32,3584]{1,0:T(8,128)(2,1)}), bf16[1024,3584]{1,0:T(8,128)(2,1)}) %all-gather.3.cloned.1.call-update) | async-done | bytes 7340048 | tf_op jit(solution)/shard_map/all_gather | solution.py:62
  88.1 7.3 %fusion.2 = f32[1024,512]{1,0:T(8,128)S(1)} fusion(bf16[1024,3584]{1,0:T(8,128)(2,1)} %all-gather.3.cloned.1.call-done, bf16[1,3584,512]{2,1,0:T(8,128)(2,1)} %param.16), kind=kOutput, calls=%fused_computation.3 | convolution fusion | flops 3758096384 | bytes 13107200 | tf_op jit(solution)/shard_map/dot_general | solution.py:66
  95.4 14.4 %convolution_convert_fusion = bf16[1024,3584]{1,0:T(8,128)(2,1)} fusion(bf16[1,512,3584]{2,1,0:T(8,128)(2,1)} %param.17, f32[1024,512]{1,0:T(8,128)S(1)} %fusion.2, bf16[1024,3584]{1,0:T(8,128)(2,1)} %all-gather.3.cloned.1.call-done, bf16[1,3584,512]{2,1,0:T(8,128)(2,1)} %param.15, f32[1024]{0:T(1024)S(1)} %bitcast.28), kind=kOutput, calls=%fused_computation.1 | convolution fusion | flops 7523532800 | bytes 24121344 | tf_op jit(solution)/shard_map/dot_general | solution.py:68
  109.8 0.0 copy-start.2
  109.8 0.0 copy-start.3
  109.8 0.0 copy-start.1
  109.8 0.0 reduce-scatter.2.cloned.1.call-update
  109.8 0.9 copy-done.2
  110.7 0.2 reshape.62
  110.9 0.0 copy-done.3
  110.9 0.1 iota_compare_fusion.1
  111.0 0.2 copy-done.1
  111.2 0.5 fusion.25
  111.7 0.5 fusion.14
  112.1 0.8 copy.21
  112.9 142.5 %reduce-scatter.2.cloned.1.call-done = bf16[32,3584]{1,0:T(8,128)(2,1)} async-done(((bf16[1024,3584]{1,0:T(8,128)(2,1)}), bf16[32,3584]{1,0:T(8,128)(2,1)}) %reduce-scatter.2.cloned.1.call-update) | async-done | bytes 229392 | tf_op jit(solution)/shard_map/reduce_scatter | solution.py:69
  (3 shorter events, 0.0 us)
Async XLA Ops:
  7.2 3.0 %copy-start = (bf16[3584,16]{0,1:T(8,128)(2,1)S(1)}, bf16[3584,16]{0,1:T(8,128)(2,1)}, u32[]{:S(2)}) copy-start(bf16[3584,16]{0,1:T(8,128)(2,1)} %param.14) | copy-start | bytes 344068
  7.2 80.9 %all-gather.3.cloned.1.call-start = ((), (), s32[]{:S(2)}) async-start(), calls=%async_computation.1 | async-start | bytes 7569408 | tf_op jit(solution)/shard_map/all_gather | solution.py:62
  10.1 245.3 %reduce-scatter.2.cloned.1.call-start = ((), (), s32[]{:S(2)}) async-start(), calls=%async_computation.2 | async-start | bytes 7569408 | tf_op jit(solution)/shard_map/reduce_scatter | solution.py:69
  109.8 0.9 copy-start.2
  109.8 1.1 copy-start.3
  109.8 1.4 copy-start.1
Sparse Core Ops, SparseCore 0:
  11.4 76.6 all-gather.2
  109.9 145.4 reduce-scatter.1

commit v2 on v0

--- a/solution.py
+++ b/solution.py
@@ -1,6 +1,10 @@
+import functools
+
 import jax
 import jax.numpy as jnp
 from jax import lax
+from jax.experimental import pallas as pl
+from jax.experimental.pallas import tpu as pltpu
 from jax.sharding import PartitionSpec as P
 
 LATENT = 512
@@ -41,6 +45,271 @@
     return (
         lax.broadcasted_iota(jnp.int32, (counts.shape[0], capacity), 1) < counts[:, None]
     ).reshape(-1)
+
+
+PLANE = 4
+GATE_LANES = 128
+LOW_LANE = 64
+COPIES = 112
+
+
+def dense_kernel(
+    depth, a0, a1, wg_hbm, wu_hbm, wd_hbm, out,
+    x0, x1, wg, wu, wd, hid, acc, so, sr, b1, r1, b2, r2, b3, r3, wsem, ssem, rsem,
+):
+    rows = a0.shape[0]
+    half = a1.shape[1]
+    me = lax.axis_index("ep")
+    side = lax.axis_index("side")
+    plane = me // PLANE
+    g0 = me % PLANE
+    x, y = g0 % 2, g0 // 2
+    gx = y * 2 + (1 - x)
+    gy = (1 - y) * 2 + x
+    gd = (1 - y) * 2 + (1 - x)
+    base = plane * PLANE
+    to_x, to_y = {"ep": base + gx}, {"ep": base + gy}
+    to_side = {"side": 1 - side}
+    to_plane = [None] + [{"ep": (plane + d) % depth * PLANE + g0} for d in range(1, depth)]
+    first, second = (to_x, to_y), (to_y, to_x)
+    near, far = (gx, gy), (gy, gx)
+    mesh_ids = pl.DeviceIdType.MESH
+    started = []
+
+    def send(src, dst, target):
+        k = len(started)
+        copy = pltpu.make_async_remote_copy(
+            src_ref=src, dst_ref=dst, send_sem=ssem.at[k], recv_sem=rsem.at[k],
+            device_id=target, device_id_type=mesh_ids,
+        )
+        copy.start()
+        started.append(copy)
+        return copy
+
+    loads = [
+        pltpu.make_async_copy(wg_hbm, wg, wsem.at[0]),
+        pltpu.make_async_copy(wu_hbm, wu, wsem.at[1]),
+        pltpu.make_async_copy(wd_hbm, wd, wsem.at[2]),
+    ]
+    for load in loads:
+        load.start()
+
+    barrier = pltpu.get_barrier_semaphore()
+    partners = [to_x, to_y, to_side] + to_plane[1:]
+    for target in partners:
+        pl.semaphore_signal(barrier, inc=1, device_id=target, device_id_type=mesh_ids)
+    pl.semaphore_wait(barrier, len(partners))
+
+    own = (a0, a1)
+    full = (x0, x1)
+    order = list(range(1, depth)) + [0]
+
+    def span(d):
+        return pl.ds(pl.multiple_of((plane + d) % depth * rows, rows), rows)
+
+    def slot(h, g, d):
+        return full[h].at[g, side, span(-d + depth)]
+
+    by_plane = {}
+    for d in range(1, depth):
+        for h in range(2):
+            by_plane[h, d] = send(own[h], slot(h, g0, 0), to_plane[d])
+    by_first, by_second, by_far, by_side = {}, {}, {}, {}
+
+    def spread(h, d):
+        block = own[h] if d == 0 else slot(h, g0, d)
+        by_first[h, d] = send(block, slot(h, g0, d), first[h])
+        by_second[h, d] = send(block, slot(h, g0, d), second[h])
+        by_side[h, 0, d] = send(block, slot(h, g0, d), to_side)
+
+    def pass_on(h, d):
+        by_first[h, d].wait_recv()
+        block = slot(h, near[h], d)
+        by_far[h, d] = send(block, block, second[h])
+        by_side[h, 1, d] = send(block, block, to_side)
+
+    for h in range(2):
+        spread(h, 0)
+        full[h][g0, side, span(0)] = own[h][...]
+    for d in range(1, depth):
+        for h in range(2):
+            by_plane[h, d].wait_recv()
+            spread(h, d)
+        for h in range(2):
+            pass_on(h, d - 1)
+    for h in range(2):
+        pass_on(h, depth - 1)
+    for d in range(depth):
+        for h in range(2):
+            by_second[h, d].wait_recv()
+            block = slot(h, far[h], d)
+            by_side[h, 2, d] = send(block, block, to_side)
+
+    lanes = lax.broadcasted_iota(jnp.int32, (1, GATE_LANES), 1)
+    mine = (lanes == me) | (lanes == me + LOW_LANE)
+
+    def both_sides(ref, g, columns):
+        return jnp.concatenate([ref[g, side, :, columns], ref[g, 1 - side, :, columns]], axis=0)
+
+    group_rows = x0.shape[2]
+    wide = 256
+    deep = 512
+
+    def compute(g):
+        tail = both_sides(x0, g, pl.ds(half, GATE_LANES)).astype(jnp.float32)
+        share = jnp.sum(jnp.where(mine, tail, 0.0), axis=1, keepdims=True)
+
+        @pl.loop(0, wg.shape[1] // wide)
+        def _(n):
+            columns = pl.ds(pl.multiple_of(n * wide, wide), wide)
+            rows0 = both_sides(x0, g, pl.ds(0, half))
+            rows1 = both_sides(x1, g, pl.ds(0, half))
+            gate = jnp.dot(rows0, wg[pl.ds(0, half), columns], preferred_element_type=jnp.float32)
+            gate += jnp.dot(rows1, wg[pl.ds(half, half), columns], preferred_element_type=jnp.float32)
+            up = jnp.dot(rows0, wu[pl.ds(0, half), columns], preferred_element_type=jnp.float32)
+            up += jnp.dot(rows1, wu[pl.ds(half, half), columns], preferred_element_type=jnp.float32)
+            hidden = gate / (1.0 + jnp.exp(-gate)) * up * share
+            hid[:, columns] = hidden.astype(jnp.bfloat16)
+
+        @pl.loop(0, wd.shape[1] // deep)
+        def _(n):
+            columns = pl.ds(pl.multiple_of(n * deep, deep), deep)
+            result = jnp.dot(hid[...], wd[:, columns], preferred_element_type=jnp.float32)
+            acc[g, :, columns] = result[:group_rows]
+            so[g, :, columns] = result[group_rows:].astype(jnp.bfloat16)
+
+        return send(so.at[g], sr.at[g], to_side)
+
+    def features(h):
+        return pl.ds(h * half, half)
+
+    def chip_sum(g, h, d):
+        part = sr[g, span(d), features(h)].astype(jnp.float32)
+        return acc[g, span(d), features(h)] + part
+
+    def f32(ref, *index):
+        return ref[index].astype(jnp.float32)
+
+    back1, back2, back3 = {}, {}, {}
+
+    def to_second(g, h, i, d):
+        b1[h, i, d] = chip_sum(g, h, d).astype(jnp.bfloat16)
+        back1[h, i, d] = send(b1.at[h, i, d], r1.at[h, i, d], second[h])
+
+    def arrived(j, halves):
+        for d in range(depth):
+            for h in halves:
+                by_side[h, j, d].wait_recv()
+
+    for load in loads:
+        load.wait()
+    arrived(0, (0, 1))
+    side0 = compute(g0)
+    arrived(1, (0,))
+    arrived(2, (1,))
+    sidex = compute(gx)
+    arrived(1, (1,))
+    arrived(2, (0,))
+    for d in range(depth):
+        for h in range(2):
+            by_far[h, d].wait_recv()
+            block = slot(h, gd, d)
+            by_side[h, 3, d] = send(block, block, to_side)
+    sidex.wait_recv()
+    for d in order:
+        to_second(gx, 1, 0, d)
+    sidey = compute(gy)
+    arrived(3, (0, 1))
+    sidey.wait_recv()
+    for d in order:
+        to_second(gy, 0, 0, d)
+    sided = compute(gd)
+    side0.wait_recv()
+    sided.wait_recv()
+    for d in order:
+        for h in range(2):
+            to_second(gd, h, 1, d)
+
+    def to_first(h, d):
+        back1[h, 1, d].wait_recv()
+        total = chip_sum(near[h], h, d) + f32(r1, h, 1, d)
+        b2[h, d] = total.astype(jnp.bfloat16)
+        back2[h, d] = send(b2.at[h, d], r2.at[h, d], first[h])
+
+    def plane_sum(h, d):
+        back1[h, 0, d].wait_recv()
+        back2[h, d].wait_recv()
+        return chip_sum(g0, h, d) + f32(r1, h, 0, d) + f32(r2, h, d)
+
+    def to_owner(h, d):
+        b3[h, d - 1] = plane_sum(h, d).astype(jnp.bfloat16)
+        back3[h, d] = send(b3.at[h, d - 1], r3.at[h, d - 1], to_plane[d])
+
+    for i, d in enumerate(order):
+        for h in range(2):
+            to_first(h, d)
+        if i > 0:
+            for h in range(2):
+                to_owner(h, order[i - 1])
+    for h in range(2):
+        total = plane_sum(h, 0)
+        for d in range(1, depth):
+            back3[h, d].wait_recv()
+            total += f32(r3, h, d - 1)
+        out[:, features(h)] = total.astype(jnp.bfloat16)
+    for copy in started:
+        copy.wait_send()
+
+
+def dense_moe(normed, dense, gate_matrix, up_matrix, down_matrix):
+    count, width = normed.shape
+    devices, experts = lax.axis_size("ep"), dense.shape[1]
+    half = width // 2
+    depth = devices // PLANE
+    high = dense.astype(jnp.bfloat16)
+    low = (dense - high.astype(jnp.float32)).astype(jnp.bfloat16)
+    pad = jnp.zeros((count, LOW_LANE - experts), jnp.bfloat16)
+    a0 = jnp.concatenate([normed[:, :half], high, pad, low, pad], axis=1)
+    a1 = normed[:, half:]
+    rows = depth * count
+    bf16 = jnp.bfloat16
+    vmem = pl.BlockSpec(memory_space=pltpu.VMEM)
+    hbm = pl.BlockSpec(memory_space=pl.ANY)
+    hidden_units = gate_matrix.shape[1]
+    return pl.pallas_call(
+        functools.partial(dense_kernel, depth),
+        out_shape=jax.ShapeDtypeStruct((count, width), bf16),
+        in_specs=[vmem, vmem, hbm, hbm, hbm],
+        out_specs=vmem,
+        scratch_shapes=[
+            pltpu.VMEM((PLANE, 2, rows, half + GATE_LANES), bf16),
+            pltpu.VMEM((PLANE, 2, rows, half), bf16),
+            pltpu.VMEM(gate_matrix.shape, bf16),
+            pltpu.VMEM(up_matrix.shape, bf16),
+            pltpu.VMEM(down_matrix.shape, bf16),
+            pltpu.VMEM((2 * rows, hidden_units), bf16),
+            pltpu.VMEM((PLANE, rows, width), jnp.float32),
+            pltpu.VMEM((PLANE, rows, width), bf16),
+            pltpu.VMEM((PLANE, rows, width), bf16),
+            pltpu.VMEM((2, 2, depth, count, half), bf16),
+            pltpu.VMEM((2, 2, depth, count, half), bf16),
+            pltpu.VMEM((2, depth, count, half), bf16),
+            pltpu.VMEM((2, depth, count, half), bf16),
+            pltpu.VMEM((2, depth - 1, count, half), bf16),
+            pltpu.VMEM((2, depth - 1, count, half), bf16),
+            pltpu.SemaphoreType.DMA((3,)),
+            pltpu.SemaphoreType.DMA((COPIES,)),
+            pltpu.SemaphoreType.DMA((COPIES,)),
+        ],
+        compiler_params=pltpu.CompilerParams(
+            collective_id=0, has_side_effects=True, vmem_limit_bytes=56 * 1024 * 1024
+        ),
+        cost_estimate=pl.CostEstimate(
+            flops=12 * PLANE * rows * width * hidden_units,
+            bytes_accessed=6 * width * hidden_units,
+            transcendentals=0,
+        ),
+    )(a0, a1, gate_matrix, up_matrix, down_matrix)
 
 
 def body(queries, latents, lengths, tokens, routes, router, gate_weight, up_weight, down_weight):
@@ -56,6 +325,10 @@
     one_hot = routes[:, :, None] == lax.broadcasted_iota(jnp.int32, (1, 1, experts), 2)
     chosen = jnp.sum(jnp.where(one_hot, affinity[:, None, :], 0.0), axis=2)
     gates = chosen / jnp.sum(chosen, axis=1, keepdims=True) * ROUTE_SCALE
+    if capacity == token_count and experts % PLANE == 0 and experts <= LOW_LANE:
+        dense = jnp.sum(jnp.where(one_hot, gates[:, :, None], 0.0), axis=1)
+        moe = dense_moe(normed, dense, gate_weight[0], up_weight[0], down_weight[0])
+        return (attended, moe)
     flat_hot = one_hot.reshape(-1, experts).astype(jnp.int32)
     slot = jnp.sum((jnp.cumsum(flat_hot, axis=0) - flat_hot) * flat_hot, axis=1)
     counts = jnp.sum(flat_hot, axis=0)

time: 284 us -> 109 us (0.38)
  the two profiles are of different devices: /device:TPU:14 before, /device:TPU:0 now
where the time goes in v2:
time: 109 us; the launch traced here: 108 us
  Pallas kernels  98.3 us (90%)
  local copies, waits for them, and re-layouts  5.14 us (5%)
  matrix products  2.42 us (2%)
  other arithmetic  1.19 us (1%)
    pallas_call x1, Pallas kernels, dense_moe(): pl.pallas_call(functools.partial(dense_kernel, depth), out_shape=jax.Shap...  98.3 us
    unnamed x10, local copies, waits for them, and re-layouts  2.48 us

profile of v2, /device:TPU:0, one launch (start us, length us, event | category | flops | bytes accessed | tf_op | source)
XLA Modules:
  0.0 107.8 jit_solution(8796965079738419434)
XLA Ops:
  0.6 0.0 copy-start
  0.6 0.0 copy-start.1
  0.7 0.8 iota_compare_fusion.1
  1.5 1.1 %reshape.62 = bf16[2,64,576]{2,1,0:T(8,128)(2,1)S(1)} reshape(bf16[2,36864]{1,0:T(2,128)(2,1)} %param.9) | data formatting | bytes 294912 | tf_op jit(solution)/shard_map/vmap()/reshape | solution.py:20
  2.6 1.8 %fusion.14 = (f32[2,64]{1,0:T(2,128)S(1)}, f32[2,64,512]{2,1,0:T(8,128)S(1)}) fusion(pred[2,512]{1,0:T(4,128)(4,1)S(1)} %iota_compare_fusion.1, bf16[2,64,576]{2,1,0:T(8,128)(2,1)S(1)} %reshape.62, bf16[2,576,512]{2,1,0:T(8,128)(2,1)} %param.10), kind=kOutput, calls=%fused_computation.28 | convolution fusion | flops 75825664 | bytes 1590784 | tf_op jit(solution)/shard_map/vmap()/sub | solution.py:25
  4.4 0.0 copy-done.1
  4.4 0.0 copy-start.2
  4.4 0.5 fusion.5
  4.9 0.0 copy-start.3
  4.9 0.8 copy.18
  5.7 0.0 copy-done.2
  5.7 0.2 fusion.10
  5.8 0.1 fusion.11
  6.0 0.7 fusion.13
  6.6 0.0 copy-done
  6.6 0.2 fusion.8
  6.8 0.0 copy-done.3
  6.9 0.1 copy.17
  7.0 0.1 copy.16
  7.1 0.7 concatenate.3.a0
  7.8 98.3 %shard_map.104 = bf16[32,3584]{1,0:T(8,128)(2,1)} custom-call(bf16[32,1920]{1,0:T(8,128)(2,1)} %concatenate.3.a0, bf16[32,1792]{1,0:T(8,128)(2,1)} %get-tuple-element.4.a1, bf16[3584,512]{1,0:T(8,128)(2,1)} %bitcast.11, bf16[3584,512]{1,0:T(8,128)(2,1)} %bitcast.12, bf16[512,3584]{1,0:T(8,128)(2,1)} %bitcast.13), custom_call_target="tpu_custom_call" | custom-call | flops 11274289152 | bytes 11010048 | tf_op jit(solution)/shard_map/pallas_call | solution.py:279
  106.1 1.6 %copy.20 = bf16[32,3584]{1,0:T(8,128)(2,1)} copy(bf16[32,3584]{1,0:T(8,128)(2,1)} %shard_map.104) | data formatting | bytes 458752
  (7 shorter events, 0.1 us)
Async XLA Ops:
  0.6 6.0 %copy-start = (bf16[3584,16]{0,1:T(8,128)(2,1)S(1)}, bf16[3584,16]{0,1:T(8,128)(2,1)}, u32[]{:S(2)}) copy-start(bf16[3584,16]{0,1:T(8,128)(2,1)} %param.14) | copy-start | bytes 344068
  0.6 3.7 %copy-start.1 = (bf16[2,576,512]{2,1,0:T(8,128)(2,1)S(1)}, bf16[2,576,512]{2,1,0:T(8,128)(2,1)}, u32[]{:S(2)}) copy-start(bf16[2,576,512]{2,1,0:T(8,128)(2,1)} %param.10) | copy-start | bytes 3538948
  4.4 1.3 %copy-start.2 = (bf16[32,3584]{1,0:T(8,128)(2,1)S(1)}, bf16[32,3584]{1,0:T(8,128)(2,1)}, u32[]{:S(2)}) copy-start(bf16[32,3584]{1,0:T(8,128)(2,1)} %param.12) | copy-start | bytes 688132
  4.9 1.9 %copy-start.3 = (s32[32,8]{0,1:T(8,128)S(1)}, s32[32,8]{0,1:T(8,128)}, u32[]{:S(2)}) copy-start(s32[32,8]{0,1:T(8,128)} %param.13) | copy-start | bytes 3076

commit v3 on v2

--- a/solution.py
+++ b/solution.py
@@ -70,7 +70,15 @@
     base = plane * PLANE
     to_x, to_y = {"ep": base + gx}, {"ep": base + gy}
     to_side = {"side": 1 - side}
-    to_plane = [None] + [{"ep": (plane + d) % depth * PLANE + g0} for d in range(1, depth)]
+    def other(d):
+        result, bit = plane, 1
+        while bit < depth:
+            if d & bit:
+                result = result + bit - plane // bit % 2 * (2 * bit)
+            bit *= 2
+        return result
+
+    to_plane = [None] + [{"ep": other(d) * PLANE + g0} for d in range(1, depth)]
     first, second = (to_x, to_y), (to_y, to_x)
     near, far = (gx, gy), (gy, gx)
     mesh_ids = pl.DeviceIdType.MESH
@@ -102,48 +110,57 @@
 
     own = (a0, a1)
     full = (x0, x1)
-    order = list(range(1, depth)) + [0]
+    order = list(range(depth - 1, -1, -1))
 
     def span(d):
-        return pl.ds(pl.multiple_of((plane + d) % depth * rows, rows), rows)
+        return pl.ds(pl.multiple_of(other(d) * rows, rows), rows)
 
     def slot(h, g, d):
-        return full[h].at[g, side, span(-d + depth)]
-
-    by_plane = {}
-    for d in range(1, depth):
+        return full[h].at[g, side, span(d)]
+
+    by_plane, by_first, by_second, by_far, by_side = {}, {}, {}, {}, {}
+
+    def across(d):
         for h in range(2):
             by_plane[h, d] = send(own[h], slot(h, g0, 0), to_plane[d])
-    by_first, by_second, by_far, by_side = {}, {}, {}, {}
-
-    def spread(h, d):
-        block = own[h] if d == 0 else slot(h, g0, d)
-        by_first[h, d] = send(block, slot(h, g0, d), first[h])
-        by_second[h, d] = send(block, slot(h, g0, d), second[h])
-        by_side[h, 0, d] = send(block, slot(h, g0, d), to_side)
-
-    def pass_on(h, d):
-        by_first[h, d].wait_recv()
-        block = slot(h, near[h], d)
-        by_far[h, d] = send(block, block, second[h])
-        by_side[h, 1, d] = send(block, block, to_side)
-
-    for h in range(2):
-        spread(h, 0)
-        full[h][g0, side, span(0)] = own[h][...]
-    for d in range(1, depth):
-        for h in range(2):
-            by_plane[h, d].wait_recv()
-            spread(h, d)
-        for h in range(2):
-            pass_on(h, d - 1)
-    for h in range(2):
-        pass_on(h, depth - 1)
-    for d in range(depth):
+
+    def spread(d):
+        for h in range(2):
+            block = own[h] if d == 0 else slot(h, g0, d)
+            by_first[h, d] = send(block, slot(h, g0, d), first[h])
+        for h in range(2):
+            block = own[h] if d == 0 else slot(h, g0, d)
+            by_second[h, d] = send(block, slot(h, g0, d), second[h])
+            by_side[h, 0, d] = send(block, slot(h, g0, d), to_side)
+
+    def pass_on(d):
+        for h in range(2):
+            by_first[h, d].wait_recv()
+            block = slot(h, near[h], d)
+            by_far[h, d] = send(block, block, second[h])
+            by_side[h, 1, d] = send(block, block, to_side)
+
+    def collect(d):
         for h in range(2):
             by_second[h, d].wait_recv()
             block = slot(h, far[h], d)
             by_side[h, 2, d] = send(block, block, to_side)
+
+    across(1)
+    across(2)
+    spread(0)
+    for h in range(2):
+        full[h][g0, side, span(0)] = own[h][...]
+    pass_on(0)
+    for d in range(1, depth):
+        for h in range(2):
+            by_plane[h, d].wait_recv()
+        if 1 < d < depth - 1:
+            across(d + 1)
+        spread(d)
+        pass_on(d)
+        collect(d - 1)
+    collect(depth - 1)
 
     lanes = lax.broadcasted_iota(jnp.int32, (1, GATE_LANES), 1)
     mine = (lanes == me) | (lanes == me + LOW_LANE)
@@ -226,9 +243,12 @@
     sided = compute(gd)
     side0.wait_recv()
     sided.wait_recv()
-    for d in order:
-        for h in range(2):
-            to_second(gd, h, 1, d)
+    def diagonal(i):
+        for h in range(2):
+            to_second(gd, h, 1, order[i])
+
+    for i in range(2):
+        diagonal(i)
 
     def to_first(h, d):
         back1[h, 1, d].wait_recv()
@@ -248,6 +268,8 @@
     for i, d in enumerate(order):
         for h in range(2):
             to_first(h, d)
+        if i + 2 < depth:
+            diagonal(i + 2)
         if i > 0:
             for h in range(2):
                 to_owner(h, order[i - 1])
@@ -325,7 +347,7 @@
     one_hot = routes[:, :, None] == lax.broadcasted_iota(jnp.int32, (1, 1, experts), 2)
     chosen = jnp.sum(jnp.where(one_hot, affinity[:, None, :], 0.0), axis=2)
     gates = chosen / jnp.sum(chosen, axis=1, keepdims=True) * ROUTE_SCALE
-    if capacity == token_count and experts % PLANE == 0 and experts <= LOW_LANE:
+    if capacity == token_count and experts in (8, 16, 32, 64) and experts <= LOW_LANE:
         dense = jnp.sum(jnp.where(one_hot, gates[:, :, None], 0.0), axis=1)
         moe = dense_moe(normed, dense, gate_weight[0], up_weight[0], down_weight[0])
         return (attended, moe)

time: 109 us -> 106 us (0.972)
  Pallas kernels: 98.3 us -> 95.9 us
    pallas_call x1, Pallas kernels: 98.3 us -> 95.9 us  [dense_moe(): pl.pallas_call(functools.partial(dense_kernel, depth), out_shape=jax.Shap...]
where the time goes in v3:
time: 106 us; the launch traced here: 105 us
  Pallas kernels  95.9 us (90%)
  local copies, waits for them, and re-layouts  5.14 us (5%)
  matrix products  2.42 us (2%)
  other arithmetic  1.19 us (1%)
    pallas_call x1, Pallas kernels, dense_moe(): pl.pallas_call(functools.partial(dense_kernel, depth), out_shape=jax.Shap...  95.9 us
    unnamed x10, local copies, waits for them, and re-layouts  2.48 us

profile of v3, /device:TPU:0, one launch (start us, length us, event | category | flops | bytes accessed | tf_op | source)
XLA Modules:
  0.0 105.4 jit_solution(14619335302080582583)
XLA Ops:
  0.6 0.0 copy-start
  0.6 0.0 copy-start.1
  0.7 0.8 iota_compare_fusion.1
  1.5 1.1 %reshape.62 = bf16[2,64,576]{2,1,0:T(8,128)(2,1)S(1)} reshape(bf16[2,36864]{1,0:T(2,128)(2,1)} %param.9) | data formatting | bytes 294912 | tf_op jit(solution)/shard_map/vmap()/reshape | solution.py:20
  2.6 1.8 %fusion.14 = (f32[2,64]{1,0:T(2,128)S(1)}, f32[2,64,512]{2,1,0:T(8,128)S(1)}) fusion(pred[2,512]{1,0:T(4,128)(4,1)S(1)} %iota_compare_fusion.1, bf16[2,64,576]{2,1,0:T(8,128)(2,1)S(1)} %reshape.62, bf16[2,576,512]{2,1,0:T(8,128)(2,1)} %param.10), kind=kOutput, calls=%fused_computation.28 | convolution fusion | flops 75825664 | bytes 1590784 | tf_op jit(solution)/shard_map/vmap()/sub | solution.py:25
  4.4 0.0 copy-done.1
  4.4 0.0 copy-start.2
  4.4 0.5 fusion.5
  4.9 0.0 copy-start.3
  4.9 0.8 copy.18
  5.7 0.0 copy-done.2
  5.7 0.2 fusion.10
  5.8 0.1 fusion.11
  6.0 0.7 fusion.13
  6.6 0.0 copy-done
  6.6 0.2 fusion.8
  6.8 0.0 copy-done.3
  6.9 0.1 copy.17
  7.0 0.1 copy.16
  7.1 0.7 concatenate.3.a0
  7.8 95.9 %shard_map.104 = bf16[32,3584]{1,0:T(8,128)(2,1)} custom-call(bf16[32,1920]{1,0:T(8,128)(2,1)} %concatenate.3.a0, bf16[32,1792]{1,0:T(8,128)(2,1)} %get-tuple-element.4.a1, bf16[3584,512]{1,0:T(8,128)(2,1)} %bitcast.11, bf16[3584,512]{1,0:T(8,128)(2,1)} %bitcast.12, bf16[512,3584]{1,0:T(8,128)(2,1)} %bitcast.13), custom_call_target="tpu_custom_call" | custom-call | flops 11274289152 | bytes 11010048 | tf_op jit(solution)/shard_map/pallas_call | solution.py:301
  103.7 1.6 %copy.20 = bf16[32,3584]{1,0:T(8,128)(2,1)} copy(bf16[32,3584]{1,0:T(8,128)(2,1)} %shard_map.104) | data formatting | bytes 458752
  (7 shorter events, 0.1 us)
Async XLA Ops:
  0.6 6.0 %copy-start = (bf16[3584,16]{0,1:T(8,128)(2,1)S(1)}, bf16[3584,16]{0,1:T(8,128)(2,1)}, u32[]{:S(2)}) copy-start(bf16[3584,16]{0,1:T(8,128)(2,1)} %param.14) | copy-start | bytes 344068
  0.6 3.7 %copy-start.1 = (bf16[2,576,512]{2,1,0:T(8,128)(2,1)S(1)}, bf16[2,576,512]{2,1,0:T(8,128)(2,1)}, u32[]{:S(2)}) copy-start(bf16[2,576,512]{2,1,0:T(8,128)(2,1)} %param.10) | copy-start | bytes 3538948
  4.4 1.3 %copy-start.2 = (bf16[32,3584]{1,0:T(8,128)(2,1)S(1)}, bf16[32,3584]{1,0:T(8,128)(2,1)}, u32[]{:S(2)}) copy-start(bf16[32,3584]{1,0:T(8,128)(2,1)} %param.12) | copy-start | bytes 688132
  4.9 1.9 %copy-start.3 = (s32[32,8]{0,1:T(8,128)S(1)}, s32[32,8]{0,1:T(8,128)}, u32[]{:S(2)}) copy-start(s32[32,8]{0,1:T(8,128)} %param.13) | copy-start | bytes 3076

commit v4 on v3

--- a/solution.py
+++ b/solution.py
@@ -227,15 +227,15 @@
     sidex = compute(gx)
     arrived(1, (1,))
     arrived(2, (0,))
-    for d in range(depth):
-        for h in range(2):
-            by_far[h, d].wait_recv()
-            block = slot(h, gd, d)
-            by_side[h, 3, d] = send(block, block, to_side)
     sidex.wait_recv()
     for d in order:
         to_second(gx, 1, 0, d)
     sidey = compute(gy)
+    for d in range(depth):
+        for h in range(2):
+            by_far[h, d].wait_recv()
+            block = slot(h, gd, d)
+            by_side[h, 3, d] = send(block, block, to_side)
     arrived(3, (0, 1))
     sidey.wait_recv()
     for d in order:

time: 106 us -> 107 us (level)
  Pallas kernels: 95.9 us -> 97.3 us
    pallas_call x1, Pallas kernels: 95.9 us -> 97.3 us  [dense_moe(): pl.pallas_call(functools.partial(dense_kernel, depth), out_shape=jax.Shap...]
where the time goes in v4:
time: 107 us
  Pallas kernels  97.3 us (91%)
  local copies, waits for them, and re-layouts  5.14 us (5%)
  matrix products  2.42 us (2%)
  other arithmetic  1.19 us (1%)
    pallas_call x1, Pallas kernels, dense_moe(): pl.pallas_call(functools.partial(dense_kernel, depth), out_shape=jax.Shap...  97.3 us
    unnamed x10, local copies, waits for them, and re-layouts  2.48 us

profile of v4, /device:TPU:0, one launch (start us, length us, event | category | flops | bytes accessed | tf_op | source)
XLA Modules:
  0.0 106.7 jit_solution(6676663550943185390)
XLA Ops:
  0.6 0.0 copy-start
  0.6 0.0 copy-start.1
  0.7 0.8 iota_compare_fusion.1
  1.5 1.1 %reshape.62 = bf16[2,64,576]{2,1,0:T(8,128)(2,1)S(1)} reshape(bf16[2,36864]{1,0:T(2,128)(2,1)} %param.9) | data formatting | bytes 294912 | tf_op jit(solution)/shard_map/vmap()/reshape | solution.py:20
  2.6 1.8 %fusion.14 = (f32[2,64]{1,0:T(2,128)S(1)}, f32[2,64,512]{2,1,0:T(8,128)S(1)}) fusion(pred[2,512]{1,0:T(4,128)(4,1)S(1)} %iota_compare_fusion.1, bf16[2,64,576]{2,1,0:T(8,128)(2,1)S(1)} %reshape.62, bf16[2,576,512]{2,1,0:T(8,128)(2,1)} %param.10), kind=kOutput, calls=%fused_computation.28 | convolution fusion | flops 75825664 | bytes 1590784 | tf_op jit(solution)/shard_map/vmap()/sub | solution.py:25
  4.4 0.0 copy-done.1
  4.4 0.0 copy-start.2
  4.4 0.5 fusion.5
  4.9 0.0 copy-start.3
  4.9 0.8 copy.18
  5.7 0.0 copy-done.2
  5.7 0.2 fusion.10
  5.8 0.1 fusion.11
  6.0 0.7 fusion.13
  6.6 0.0 copy-done
  6.6 0.2 fusion.8
  6.8 0.0 copy-done.3
  6.9 0.1 copy.17
  7.0 0.1 copy.16
  7.1 0.7 concatenate.3.a0
  7.8 97.3 %shard_map.104 = bf16[32,3584]{1,0:T(8,128)(2,1)} custom-call(bf16[32,1920]{1,0:T(8,128)(2,1)} %concatenate.3.a0, bf16[32,1792]{1,0:T(8,128)(2,1)} %get-tuple-element.4.a1, bf16[3584,512]{1,0:T(8,128)(2,1)} %bitcast.11, bf16[3584,512]{1,0:T(8,128)(2,1)} %bitcast.12, bf16[512,3584]{1,0:T(8,128)(2,1)} %bitcast.13), custom_call_target="tpu_custom_call" | custom-call | flops 11274289152 | bytes 11010048 | tf_op jit(solution)/shard_map/pallas_call | solution.py:301
  105.1 1.6 %copy.20 = bf16[32,3584]{1,0:T(8,128)(2,1)} copy(bf16[32,3584]{1,0:T(8,128)(2,1)} %shard_map.104) | data formatting | bytes 458752
  (7 shorter events, 0.1 us)
Async XLA Ops:
  0.6 6.0 %copy-start = (bf16[3584,16]{0,1:T(8,128)(2,1)S(1)}, bf16[3584,16]{0,1:T(8,128)(2,1)}, u32[]{:S(2)}) copy-start(bf16[3584,16]{0,1:T(8,128)(2,1)} %param.14) | copy-start | bytes 344068
  0.6 3.7 %copy-start.1 = (bf16[2,576,512]{2,1,0:T(8,128)(2,1)S(1)}, bf16[2,576,512]{2,1,0:T(8,128)(2,1)}, u32[]{:S(2)}) copy-start(bf16[2,576,512]{2,1,0:T(8,128)(2,1)} %param.10) | copy-start | bytes 3538948
  4.4 1.3 %copy-start.2 = (bf16[32,3584]{1,0:T(8,128)(2,1)S(1)}, bf16[32,3584]{1,0:T(8,128)(2,1)}, u32[]{:S(2)}) copy-start(bf16[32,3584]{1,0:T(8,128)(2,1)} %param.12) | copy-start | bytes 688132
  4.9 1.9 %copy-start.3 = (s32[32,8]{0,1:T(8,128)S(1)}, s32[32,8]{0,1:T(8,128)}, u32[]{:S(2)}) copy-start(s32[32,8]{0,1:T(8,128)} %param.13) | copy-start | bytes 3076
